TPU v7x, 1024 devices: a whole 4x4x32 slice. The times are simulated.
1024 devices in a mesh: row: 4 (over x), col: 256 (over y, z, core).
Axes of the slice: x: 4, y: 4, z: 32, core: 2. Of those that a mesh axis runs over, the one named last changes fastest.
Arguments:
- tokens: bfloat16 [256, 8192], P('col', 'row'), may hold values from -6 to 6
- out_grad: bfloat16 [256, 8192], P('col', 'row'), may hold values from -1.5 to 1.5
- gate_weight: bfloat16 [8192, 28672], P('row', 'col'), may hold values from -0.0625 to 0.0625
- up_weight: bfloat16 [8192, 28672], P('row', 'col'), may hold values from -0.0625 to 0.0625
- down_weight: bfloat16 [8192, 28672], P('row', 'col'), may hold values from -0.0625 to 0.0625
Outputs:
- in_grad: bfloat16 [256, 8192], P('col', 'row')
- gate_grad: bfloat16 [8192, 28672], P('row', 'col')
- up_grad: bfloat16 [8192, 28672], P('row', 'col')
- down_grad: bfloat16 [8192, 28672], P('row', 'col')
All inputs are finite; a program needn't handle non-finite values.
Results may differ from a plain program's by a relative error of at most 0.005.
Values may be sent and summed in bfloat16 or wider, within the bound.
A program may use at most 32 MiB of HBM per device.

v0:
```python
import jax
import jax.numpy as jnp
from jax import lax
from jax.sharding import PartitionSpec as P


def contract_rows(left, right):
    return lax.dot_general(
        left, right, (((0,), (0,)), ((), ())), preferred_element_type=jnp.float32
    )


def contract_cols(left, right):
    return lax.dot_general(
        left, right, (((1,), (1,)), ((), ())), preferred_element_type=jnp.float32
    )


def elementwise(gate, up, hidden_grad):
    sig = 1.0 / (1.0 + jnp.exp(-gate))
    silu = gate * sig
    hidden = (silu * up).astype(jnp.bfloat16)
    up_delta = (hidden_grad * silu).astype(jnp.bfloat16)
    gate_delta = (hidden_grad * up * sig * (1.0 + gate * (1.0 - sig))).astype(jnp.bfloat16)
    return (hidden, gate_delta, up_delta)


def body(tokens, out_grad, gate_weight, up_weight, down_weight):
    all_tokens, all_grads = (
        lax.all_gather(tokens, "col", axis=0, tiled=True),
        lax.all_gather(out_grad, "col", axis=0, tiled=True),
    )
    gate_part = jnp.dot(all_tokens, gate_weight, preferred_element_type=jnp.float32)
    up_part = jnp.dot(all_tokens, up_weight, preferred_element_type=jnp.float32)
    grad_part = jnp.dot(all_grads, down_weight, preferred_element_type=jnp.float32)
    gate, up, hidden_grad = (
        lax.psum_scatter(gate_part, "row", scatter_dimension=0, tiled=True),
        lax.psum_scatter(up_part, "row", scatter_dimension=0, tiled=True),
        lax.psum_scatter(grad_part, "row", scatter_dimension=0, tiled=True),
    )
    hidden, gate_delta, up_delta = elementwise(gate, up, hidden_grad)
    hidden_all, gate_all, up_all = (
        lax.all_gather(hidden, "row", axis=0, tiled=True),
        lax.all_gather(gate_delta, "row", axis=0, tiled=True),
        lax.all_gather(up_delta, "row", axis=0, tiled=True),
    )
    in_grad = lax.psum_scatter(
        contract_cols(gate_all, gate_weight) + contract_cols(up_all, up_weight),
        "col",
        scatter_dimension=0,
        tiled=True,
    ).astype(jnp.bfloat16)
    down_grad = contract_rows(all_grads, hidden_all).astype(jnp.bfloat16)
    gate_grad = contract_rows(all_tokens, gate_all).astype(jnp.bfloat16)
    up_grad = contract_rows(all_tokens, up_all).astype(jnp.bfloat16)
    return (in_grad, gate_grad, up_grad, down_grad)


def solution(mesh):
    placed = (P("col", "row"), P("col", "row"), P("row", "col"), P("row", "col"), P("row", "col"))
    return jax.shard_map(
        body,
        mesh=mesh,
        in_specs=placed,
        out_specs=(P("col", "row"), P("row", "col"), P("row", "col"), P("row", "col")),
        check_vma=False,
    )
```

profile of v0, /device:TPU:4, one launch (start us, length us, event | category | flops | bytes accessed | tf_op | source)
XLA Modules:
  0.0 1684.7 jit_solution(17980512128664380471)
XLA Ops:
  7.2 0.7 all-gather.5.cloned.1.call-update
  8.0 0.7 all-gather.7.cloned.1.call-update
  8.7 265.6 %all-gather.5.cloned.1.call-done = bf16[256,1,2048]{2,1,0:T(2,128)(2,1)} async-done(((bf16[1,1,2048]{2,1,0:T(2,128)(2,1)}), bf16[256,1,2048]{2,1,0:T(2,128)(2,1)}) %all-gather.5.cloned.1.call-update) | async-done | bytes 1048592 | tf_op jit(solution)/shard_map/all_gather | solution.py:31
  274.3 3.0 fusion.10
  277.4 245.9 %all-gather.7.cloned.1.call-done = bf16[256,1,2048]{2,1,0:T(2,128)(2,1)} async-done(((bf16[1,1,2048]{2,1,0:T(2,128)(2,1)}), bf16[256,1,2048]{2,1,0:T(2,128)(2,1)}) %all-gather.7.cloned.1.call-update) | async-done | bytes 1048592 | tf_op jit(solution)/shard_map/all_gather | solution.py:30
  523.3 2.2 copy.10
  525.5 1.1 fusion.5
  526.6 0.0 reduce-scatter.6.cloned.1.call-start
  526.7 1.1 fusion.7
  527.8 1.3 dynamic-slice
  529.1 25.1 %reduce-scatter.4.cloned.1.call-done = f32[64,112]{1,0:T(8,128)} async-done(((f32[256,112]{1,0:T(8,128)}), f32[64,112]{1,0:T(8,128)}) %reduce-scatter.4.cloned.1.call-update) | async-done | bytes 28688 | tf_op jit(solution)/shard_map/reduce_scatter | solution.py:39
  554.2 42.4 %reduce-scatter.8.cloned.1.call-done = f32[64,112]{1,0:T(8,128)} async-done(((f32[256,112]{1,0:T(8,128)}), f32[64,112]{1,0:T(8,128)}) %reduce-scatter.8.cloned.1.call-update) | async-done | bytes 28688 | tf_op jit(solution)/shard_map/reduce_scatter | solution.py:37
  596.6 42.0 %reduce-scatter.6.cloned.1.call-done = f32[64,112]{1,0:T(8,128)} async-done(((f32[256,112]{1,0:T(8,128)}), f32[64,112]{1,0:T(8,128)}) %reduce-scatter.6.cloned.1.call-update) | async-done | bytes 28688 | tf_op jit(solution)/shard_map/reduce_scatter | solution.py:38
  638.6 0.8 multiply_convert_fusion
  639.4 11.9 all_gather.17
  651.3 1.1 fusion
  652.4 0.4 fusion.15
  652.8 11.9 all_gather.19
  664.7 11.9 all_gather.18
  676.5 1.1 fusion.1
  677.6 0.4 convolution_add_fusion
  678.1 995.0 %all-reduce.2 = bf16[256,2048]{1,0:T(8,128)(2,1)} all-reduce(f32[256,2048]{1,0:T(8,128)S(1)} %convolution_add_fusion), channel_id=5, replica_groups=mesh['row'=4,'col'=256] {'col'}, use_global_device_ids=true, to_apply=%region_3.0.clone | all-reduce | flops 524288 | bytes 3145728
  1673.1 1.9 dynamic-slice_convert_fusion
  1675.0 3.1 fusion.2
  (11 shorter events, 0.2 us)
Async XLA Ops:
  7.2 518.3 %copy-start = (bf16[2048,112]{0,1:T(8,128)(2,1)S(1)}, bf16[2048,112]{0,1:T(8,128)(2,1)}, u32[]{:S(2)}) copy-start(bf16[2048,112]{0,1:T(8,128)(2,1)} %param.7) | copy-start | bytes 1376260
  7.2 267.1 %all-gather.5.cloned.1.call-start = ((), (), s32[]{:S(2)}) async-start(), calls=%async_computation.6 | async-start | bytes 2105344 | tf_op jit(solution)/shard_map/all_gather | solution.py:31
  7.9 515.4 %all-gather.7.cloned.1.call-start = ((), (), s32[]{:S(2)}) async-start(), calls=%async_computation.7 | async-start | bytes 2105344 | tf_op jit(solution)/shard_map/all_gather | solution.py:30
  8.7 545.5 %reduce-scatter.4.cloned.1.call-start = ((), (), s32[]{:S(2)}) async-start(), calls=%async_computation.3 | async-start | bytes 163840 | tf_op jit(solution)/shard_map/reduce_scatter | solution.py:39
  277.4 249.3 %copy-start.1 = (bf16[2048,112]{0,1:T(8,128)(2,1)S(1)}, bf16[2048,112]{0,1:T(8,128)(2,1)}, u32[]{:S(2)}) copy-start(bf16[2048,112]{0,1:T(8,128)(2,1)} %param.8) | copy-start | bytes 1376260
  277.4 319.2 %reduce-scatter.8.cloned.1.call-start = ((), (), s32[]{:S(2)}) async-start(), calls=%async_computation.5 | async-start | bytes 163840 | tf_op jit(solution)/shard_map/reduce_scatter | solution.py:37
  526.6 112.0 %reduce-scatter.6.cloned.1.call-start = ((), (), s32[]{:S(2)}) async-start(), calls=%async_computation.4 | async-start | bytes 163840 | tf_op jit(solution)/shard_map/reduce_scatter | solution.py:38
Sparse Core Ops, SparseCore 0:
  12.2 262.1 all-gather.4
  278.4 244.8 all-gather.6
  527.2 26.8 reduce-scatter.3
  558.3 38.1 reduce-scatter.7
  600.4 38.1 reduce-scatter.5
where the time goes:
time: 1690 us; the launch traced here: 1680 us
  blocking collectives  1030 us (61%)
  waiting for transfers between devices  622 us (37%)
    unnamed x1, blocking collectives  995 us
    all_gather x1, waiting for transfers between devices, body(): lax.all_gather(out_grad, 'col', axis=0, tiled=True)  266 us
    all_gather x1, waiting for transfers between devices, body(): lax.all_gather(tokens, 'col', axis=0, tiled=True)  246 us
    reduce_scatter x1, waiting for transfers between devices, body(): lax.psum_scatter(gate_part, 'row', scatter_dimension=0, tiled=True)  42.4 us
    reduce_scatter x1, waiting for transfers between devices, body(): lax.psum_scatter(up_part, 'row', scatter_dimension=0, tiled=True)  42 us
  transfers between devices with their start and end apart: 5, of which 5 were waited for; matrix products, arithmetic and copies ran while one was open for 1% of the time, Pallas kernels for 0%

commit v1 on v0

v1 whole, which is shorter than its diff:
```python
import functools

import jax
import jax.numpy as jnp
from jax import lax
from jax.experimental import pallas as pl
from jax.experimental.pallas import tpu as pltpu
from jax.sharding import PartitionSpec as P

MESH = pl.DeviceIdType.MESH
F32, BF16 = jnp.float32, jnp.bfloat16
NY, NZ = 4, 32

KS = (0, 1, -1, 2, -2, 3, -3, 4)
SS = (0, -1, 1, 2)
CHUNKS = 4


def slot(k, core, dy, s):
    return ((KS.index(k) * 2 + core) * 4 + dy) * 4 + SS.index(s)


def spreads(k):
    out = [(s, k, s) for s in (-1, 1, 2)]
    if k == 3:
        out += [(3, 4, -1), (4, 4, 0)]
    if k == -3:
        out += [(-3, 4, 1), (-2, 4, 2)]
    return out


def near_far(k, s):
    dz = -(4 * k + s) % NZ
    dz = dz - NZ if dz > 16 else dz
    for low, high, f in ((-4, 3, 0), (4, 11, 8), (-12, -5, -8), (12, 16, 12), (-15, -13, -12)):
        if low <= dz <= high:
            return dz - f, f
    raise ValueError(dz)


FARS = (8, -8, 12, -12)
NEAR = {}
for _k in KS:
    for _s in SS:
        _r, _f = near_far(_k, _s)
        NEAR.setdefault(_r, []).append((_f, _k, _s))
RS = tuple(sorted(r for r in NEAR if r))
PARTNERS = (
    [(d, 0, 0, 0) for d in (1, 2, 3)]
    + [(0, d, 0, 0) for d in (1, 2, 3)]
    + [(0, 0, d, 0) for d in (-4, -3, -2, -1, 1, 2, 3, 4)]
    + [(0, 0, 0, 1)]
)


def kernel(
    tok_ref, grd_ref, gate_ref, up_ref, down_ref,
    in_ref, gate_out, up_out, down_out,
    own32, G, F, At, Ag, WT, part, XR, D, Pm, S1, R1, S2, R2, S3, R3, S4, R4, GW,
    zs, zr, ys, yr, cs, cr, xs, xrs, ds_, dr, s1s, s1r, s2s, s2r, s3s, s3r, s4s, s4r, wl, wo,
):
    x = lax.axis_index("row")
    col = lax.axis_index("col")
    core, z, y = col % 2, (col // 2) % NZ, col // (2 * NZ)

    def peer(dx, dy, dz, dc):
        return (
            (x + dx + 4) % 4,
            (((y + dy + NY) % NY) * NZ + (z + dz + NZ) % NZ) * 2 + (core + dc) % 2,
        )

    sends = []

    def copy(src, dst, ssem, rsem, to):
        return pltpu.make_async_remote_copy(
            src_ref=src, dst_ref=dst, send_sem=ssem, recv_sem=rsem, device_id=to, device_id_type=MESH
        )

    def send(src, dst, ssem, rsem, to):
        c = copy(src, dst, ssem, rsem, to)
        c.start()
        sends.append(c)

    def arrived(buf, sem):
        copy(buf, buf, sem, sem, peer(0, 0, 0, 1)).wait_recv()

    barrier = pltpu.get_barrier_semaphore()
    for p in PARTNERS:
        pl.semaphore_signal(barrier, inc=1, device_id=peer(*p), device_id_type=MESH)

    loads = [
        pltpu.make_async_copy(ref, WT.at[pl.ds(128 * i, 112)], wl.at[i])
        for i, ref in enumerate((gate_ref, up_ref, down_ref))
    ]
    for c in loads:
        c.start()
    for i in range(3):
        WT[128 * i + 112:128 * i + 128, :] = jnp.zeros((16, 2048), BF16)

    for i, ref in enumerate((tok_ref, grd_ref)):
        row = ref[...].astype(F32)
        for n in range(16):
            own32[16 * i + n:16 * i + n + 1, :] = row[:, 128 * n:128 * n + 128]
    G[0] = own32[...].astype(BF16)

    pl.semaphore_wait(barrier, len(PARTNERS))

    def zslot(k, s):
        return G.at[slot(k, 0, 0, s)]

    def zsem(k, s):
        return KS.index(k) * 4 + SS.index(s)

    def z_send(step, src, k, s):
        i = zsem(k, s)
        send(src, zslot(k, s), zs.at[i], zr.at[i], peer(0, 0, step, 0))

    def z_wait(k, s):
        arrived(zslot(k, s), zr.at[zsem(k, s)])

    def relay(k):
        if 0 <= k < 3:
            z_send(4, zslot(k, 0), k + 1, 0)
        if -3 < k <= 0:
            z_send(-4, zslot(k, 0), k - 1, 0)

    def spread(k):
        for step, k2, s in spreads(k):
            z_send(step, zslot(k, 0), k2, s)

    def y_send(k):
        for s in SS:
            if s != 0 or k == 4:
                z_wait(k, s)
        i = KS.index(k)
        for d in (1, 2, 3):
            send(
                G.at[pl.ds(slot(k, 0, 0, 0), 4)], G.at[pl.ds(slot(k, 0, d, 0), 4)],
                ys.at[i * 3 + d - 1], yr.at[i * 3 + d - 1], peer(0, d, 0, 0),
            )

    def c_send(k):
        i = KS.index(k)
        for d in (1, 2, 3):
            arrived(G.at[pl.ds(slot(k, 0, d, 0), 4)], yr.at[i * 3 + d - 1])
        send(
            G.at[pl.ds(slot(k, 0, 0, 0), 16)], G.at[pl.ds(slot(k, 1, 0, 0), 16)],
            cs.at[i], cr.at[i], peer(0, 0, 0, 1),
        )

    def rows_in_place(k):
        i = KS.index(k)
        arrived(G.at[pl.ds(slot(k, 1, 0, 0), 16)], cr.at[i])
        for c in (0, 1):
            first = slot(k, c, 0, 0)
            F[c] = G[first:first + 16].astype(F32).reshape(512, 128)
            for n in range(16):
                cols = slice(128 * n, 128 * n + 128)
                At[first:first + 16, cols] = F[c, pl.ds(n, 16, stride=32), :].astype(BF16)
                Ag[first:first + 16, cols] = F[c, pl.ds(16 + n, 16, stride=32), :].astype(BF16)

    def forward(i):
        rows = slice(64 * i, 64 * i + 64)
        nt = (((1,), (1,)), ((), ()))
        gu = lax.dot_general(At[rows, :], WT[0:256, :], nt, preferred_element_type=F32)
        hg = lax.dot_general(Ag[rows, :], WT[256:384, :], nt, preferred_element_type=F32)
        part[i, :, :, 0:256] = gu.reshape(4, 16, 256)
        part[i, :, :, 256:384] = hg.reshape(4, 16, 128)
        for d in (1, 2, 3):
            send(
                part.at[i, (x + d) % 4], XR.at[i, d - 1],
                xs.at[i * 3 + d - 1], xrs.at[i * 3 + d - 1], peer(d, 0, 0, 0),
            )

    def activate(i):
        for d in (1, 2, 3):
            arrived(XR.at[i, d - 1], xrs.at[i * 3 + d - 1])
        total = part[i, x] + XR[i, 0] + XR[i, 1] + XR[i, 2]
        gate, up, hidden_grad = total[:, 0:128], total[:, 128:256], total[:, 256:384]
        sig = 1.0 / (1.0 + jnp.exp(-gate))
        silu = gate * sig
        D[i, x, :, 0:128] = (hidden_grad * up * sig * (1.0 + gate * (1.0 - sig))).astype(BF16)
        D[i, x, :, 128:256] = (hidden_grad * silu).astype(BF16)
        D[i, x, :, 256:384] = (silu * up).astype(BF16)
        for d in (1, 2, 3):
            send(
                D.at[i, x], D.at[i, x],
                ds_.at[i * 3 + d - 1], dr.at[i * 3 + d - 1], peer(d, 0, 0, 0),
            )

    def back(i):
        for d in (1, 2, 3):
            arrived(D.at[i, (x - d + 4) % 4], dr.at[i * 3 + d - 1])
        delta = D[i, :, :, 0:256].reshape(64, 256)
        for n in range(8):
            out = jnp.dot(delta, WT[0:256, 256 * n:256 * n + 256], preferred_element_type=F32)
            for h in (0, 1):
                Pm[pl.ds(1024 * i + 2 * n + h, 64, stride=16), :] = out[:, 128 * h:128 * h + 128]
        for j in (2 * i, 2 * i + 1):
            S1[j] = Pm[512 * j + 256:512 * j + 512, :].astype(BF16)
            send(S1.at[j], R1.at[j], s1s.at[j], s1r.at[j], peer(0, 0, 0, 1))

    def over_y(i):
        for j in (0, 1):
            k = 2 * i + j
            arrived(R1.at[k], s1r.at[k])
            both = Pm[512 * k:512 * k + 256, :] + R1[k].astype(F32)
            Pm[512 * k:512 * k + 64, :] = both[0:64]
            for d in (1, 2, 3):
                S2[i, d - 1, 64 * j:64 * j + 64, :] = both[64 * d:64 * d + 64].astype(BF16)
        for d in (1, 2, 3):
            send(
                S2.at[i, d - 1], R2.at[i, d - 1],
                s2s.at[i * 3 + d - 1], s2r.at[i * 3 + d - 1], peer(0, -d, 0, 0),
            )

    def after_y(i):
        for d in (1, 2, 3):
            arrived(R2.at[i, d - 1], s2r.at[i * 3 + d - 1])
        for j in (0, 1):
            k = 2 * i + j
            total = Pm[512 * k:512 * k + 64, :]
            for d in (1, 2, 3):
                total = total + R2[i, d - 1, 64 * j:64 * j + 64, :].astype(F32)
            for n, s in enumerate(SS):
                piece = total[16 * n:16 * n + 16]
                r, f = near_far(KS[k], s)
                if r == 0:
                    Pm[512 * k + 16 * n:512 * k + 16 * n + 16, :] = piece
                else:
                    at = NEAR[r].index((f, KS[k], s))
                    S3[RS.index(r), 16 * at:16 * at + 16, :] = piece.astype(BF16)

    def held(k, s):
        at = 512 * KS.index(k) + 16 * SS.index(s)
        return Pm[at:at + 16, :]

    def at_relay(f):
        total = None
        for r, entries in NEAR.items():
            for n, (f2, k, s) in enumerate(entries):
                if f2 == f:
                    term = held(k, s) if r == 0 else R3[RS.index(r), 16 * n:16 * n + 16, :].astype(F32)
                    total = term if total is None else total + term
        return total

    relay(0)
    spread(0)
    for k in (1, -1):
        z_wait(k, 0)
        relay(k)
        spread(k)
    y_send(0)
    for k in (2, -2):
        z_wait(k, 0)
        relay(k)
        spread(k)
    for k in (1, -1):
        y_send(k)
    c_send(0)
    for k in (3, -3):
        z_wait(k, 0)
        spread(k)
    for k in (2, -2):
        y_send(k)
    for k in (1, -1):
        c_send(k)
    for c in loads:
        c.wait()
    for k in (0, 1):
        rows_in_place(k)
    forward(0)
    for k in (2, -2):
        c_send(k)
    for k in (3, -3, 4):
        y_send(k)
    for k in (-1, 2):
        rows_in_place(k)
    forward(1)
    activate(0)
    for k in (3, -3, 4):
        c_send(k)
    for k in (-2, 3):
        rows_in_place(k)
    forward(2)
    for k in (-3, 4):
        rows_in_place(k)
    forward(3)
    activate(1)
    back(0)
    activate(2)
    activate(3)
    back(1)
    over_y(0)
    back(2)
    over_y(1)
    over_y(2)
    back(3)
    over_y(3)
    for i in range(CHUNKS):
        after_y(i)
    for i, r in enumerate(RS):
        n = 16 * len(NEAR[r])
        send(S3.at[i, pl.ds(0, n)], R3.at[i, pl.ds(0, n)], s3s.at[i], s3r.at[i], peer(0, 0, r, 0))
    for i, r in enumerate(RS):
        arrived(R3.at[i, pl.ds(0, 16 * len(NEAR[r]))], s3r.at[i])
    for i, f in enumerate(FARS):
        S4[i] = at_relay(f)
        send(S4.at[i], R4.at[i], s4s.at[i], s4r.at[i], peer(0, 0, f, 0))

    tn = (((0,), (0,)), ((), ()))
    deltas = D[:, :, :, 0:256].reshape(256, 256)
    hidden = D[:, :, :, 256:384].reshape(256, 128)
    for n in range(8):
        cols = slice(256 * n, 256 * n + 256)
        GW[0:256, cols] = lax.dot_general(deltas, At[:, cols], tn, preferred_element_type=F32).astype(BF16)
        GW[256:384, cols] = lax.dot_general(hidden, Ag[:, cols], tn, preferred_element_type=F32).astype(BF16)
    stores = [
        pltpu.make_async_copy(GW.at[pl.ds(128 * i, 112)], ref, wo.at[i])
        for i, ref in enumerate((gate_out, up_out, down_out))
    ]
    for c in stores:
        c.start()
    mine = at_relay(0)
    for i in range(4):
        arrived(R4.at[i], s4r.at[i])
        mine = mine + R4[i]
    for n in range(16):
        in_ref[:, 128 * n:128 * n + 128] = mine[n:n + 1, :].astype(BF16)
    for c in sends:
        c.wait_send()
    for c in stores:
        c.wait()


def body(tokens, out_grad, gate_weight, up_weight, down_weight):
    vmem = pl.BlockSpec(memory_space=pltpu.VMEM)
    anywhere = pl.BlockSpec(memory_space=pl.ANY)
    wide = jax.ShapeDtypeStruct((112, 2048), BF16)
    dma = lambda n: pltpu.SemaphoreType.DMA((n,))
    in_grad, gate_grad, up_grad, down_grad = pl.pallas_call(
        kernel,
        name="swiglu_backward",
        out_shape=(jax.ShapeDtypeStruct((1, 2048), BF16), wide, wide, wide),
        in_specs=[vmem, vmem, anywhere, anywhere, anywhere],
        out_specs=(vmem, anywhere, anywhere, anywhere),
        scratch_shapes=[
            pltpu.VMEM((32, 128), F32),
            pltpu.VMEM((256, 32, 128), BF16),
            pltpu.VMEM((2, 512, 128), F32),
            pltpu.VMEM((256, 2048), BF16),
            pltpu.VMEM((256, 2048), BF16),
            pltpu.VMEM((384, 2048), BF16),
            pltpu.VMEM((4, 4, 16, 384), F32),
            pltpu.VMEM((4, 3, 16, 384), F32),
            pltpu.VMEM((4, 4, 16, 384), BF16),
            pltpu.VMEM((4096, 128), F32),
            pltpu.VMEM((8, 256, 128), BF16),
            pltpu.VMEM((8, 256, 128), BF16),
            pltpu.VMEM((4, 3, 128, 128), BF16),
            pltpu.VMEM((4, 3, 128, 128), BF16),
            pltpu.VMEM((len(RS), 64, 128), BF16),
            pltpu.VMEM((len(RS), 64, 128), BF16),
            pltpu.VMEM((4, 16, 128), F32),
            pltpu.VMEM((4, 16, 128), F32),
            pltpu.VMEM((384, 2048), BF16),
            dma(32), dma(32), dma(24), dma(24), dma(8), dma(8), dma(12), dma(12), dma(12), dma(12),
            dma(8), dma(8), dma(12), dma(12), dma(len(RS)), dma(len(RS)), dma(4), dma(4), dma(3), dma(3),
        ],
        compiler_params=pltpu.CompilerParams(
            collective_id=0, has_side_effects=True, vmem_limit_bytes=48 * 2 ** 20
        ),
    )(tokens, out_grad, gate_weight.T, up_weight.T, down_weight.T)
    return in_grad, gate_grad.T, up_grad.T, down_grad.T


def solution(mesh):
    placed = (P("col", "row"), P("col", "row"), P("row", "col"), P("row", "col"), P("row", "col"))
    return jax.shard_map(
        body,
        mesh=mesh,
        in_specs=placed,
        out_specs=(P("col", "row"), P("row", "col"), P("row", "col"), P("row", "col")),
        check_vma=False,
    )
```

time: 1690 us -> 89.1 us (0.05)
  the two profiles are of different devices: /device:TPU:4 before, /device:TPU:8 now
where the time goes in v1:
time: 89.1 us; the launch traced here: 88.8 us
  Pallas kernels  80.8 us (91%)
  local copies, waits for them, and re-layouts  7.34 us (8%)
    pallas_call x1, Pallas kernels, body(): pl.pallas_call(kernel, name='swiglu_backward', out_shape=(jax.ShapeDtypeS...  80.8 us
    unnamed x14, local copies, waits for them, and re-layouts  7.34 us

profile of v1, /device:TPU:8, one launch (start us, length us, event | category | flops | bytes accessed | tf_op | source)
XLA Modules:
  0.0 88.8 jit_solution(1742129003681677691)
XLA Ops:
  0.6 0.0 copy-start
  0.6 1.0 %copy-done = bf16[2048,112]{0,1:T(8,128)(2,1)S(1)} copy-done((bf16[2048,112]{0,1:T(8,128)(2,1)S(1)}, bf16[2048,112]{0,1:T(8,128)(2,1)}, u32[]{:S(2)}) %copy-start) | copy-done | bytes 458776
  1.7 0.0 copy-start.1
  1.7 1.0 %copy-done.1 = bf16[2048,112]{0,1:T(8,128)(2,1)S(1)} copy-done((bf16[2048,112]{0,1:T(8,128)(2,1)S(1)}, bf16[2048,112]{0,1:T(8,128)(2,1)}, u32[]{:S(2)}) %copy-start.1) | copy-done | bytes 458776
  2.7 0.0 copy-start.2
  2.7 1.0 %copy-done.2 = bf16[2048,112]{0,1:T(8,128)(2,1)S(1)} copy-done((bf16[2048,112]{0,1:T(8,128)(2,1)S(1)}, bf16[2048,112]{0,1:T(8,128)(2,1)}, u32[]{:S(2)}) %copy-start.2) | copy-done | bytes 458776
  3.7 0.0 copy-start.3
  3.7 0.7 copy-done.3
  4.4 0.0 copy-start.4
  4.4 0.7 copy-done.4
  5.1 80.8 %swiglu_backward.1 = (bf16[1,2048]{1,0:T(2,128)(2,1)S(1)}, bf16[112,2048]{1,0:T(8,128)(2,1)S(1)}, bf16[112,2048]{1,0:T(8,128)(2,1)S(1)}, bf16[112,2048]{1,0:T(8,128)(2,1)S(1)}) custom-call(bf16[1,2048]{1,0:T(2,128)(2,1)S(1)} %copy-done.3, bf16[1,2048]{1,0:T(2,128)(2,1)S(1)} %copy-done.4, bf16[112,2048]{1,0:T(8,128)(2,1)S(1)} %bitcast.9, ...), custom_call_target="tpu_custom_call" | custom-call | tf_op jit(solution)/shard_map/swiglu_backward/pallas_call | solution.py:341
  85.9 0.6 copy.13
  86.5 0.8 copy.14
  87.2 0.8 copy.15
  88.0 0.8 copy.16
Async XLA Ops:
  0.6 1.0 %copy-start = (bf16[2048,112]{0,1:T(8,128)(2,1)S(1)}, bf16[2048,112]{0,1:T(8,128)(2,1)}, u32[]{:S(2)}) copy-start(bf16[2048,112]{0,1:T(8,128)(2,1)} %param.7) | copy-start | bytes 1376260
  1.7 1.0 %copy-start.1 = (bf16[2048,112]{0,1:T(8,128)(2,1)S(1)}, bf16[2048,112]{0,1:T(8,128)(2,1)}, u32[]{:S(2)}) copy-start(bf16[2048,112]{0,1:T(8,128)(2,1)} %param.8) | copy-start | bytes 1376260
  2.7 1.0 %copy-start.2 = (bf16[2048,112]{0,1:T(8,128)(2,1)S(1)}, bf16[2048,112]{0,1:T(8,128)(2,1)}, u32[]{:S(2)}) copy-start(bf16[2048,112]{0,1:T(8,128)(2,1)} %param.9) | copy-start | bytes 1376260
  3.7 0.7 copy-start.3
  4.4 0.7 copy-start.4

commit v2 on v1

--- a/solution.py
+++ b/solution.py
@@ -56,7 +56,7 @@
 def kernel(
     tok_ref, grd_ref, gate_ref, up_ref, down_ref,
     in_ref, gate_out, up_out, down_out,
-    own32, G, F, At, Ag, WT, part, XR, D, Pm, S1, R1, S2, R2, S3, R3, S4, R4, GW,
+    rows, own32, G, F, At, Ag, WT, part, XR, D, Pm, S1, R1, S2, R2, S3, R3, S4, R4, GW,
     zs, zr, ys, yr, cs, cr, xs, xrs, ds_, dr, s1s, s1r, s2s, s2r, s3s, s3r, s4s, s4r, wl, wo,
 ):
     x = lax.axis_index("row")
@@ -84,21 +84,21 @@
     def arrived(buf, sem):
         copy(buf, buf, sem, sem, peer(0, 0, 0, 1)).wait_recv()
 
+    inputs = [
+        pltpu.make_async_copy(ref, rows.at[i], wl.at[3 + i]) for i, ref in enumerate((tok_ref, grd_ref))
+    ]
+    for c in inputs:
+        c.start()
     barrier = pltpu.get_barrier_semaphore()
     for p in PARTNERS:
         pl.semaphore_signal(barrier, inc=1, device_id=peer(*p), device_id_type=MESH)
 
-    loads = [
-        pltpu.make_async_copy(ref, WT.at[pl.ds(128 * i, 112)], wl.at[i])
-        for i, ref in enumerate((gate_ref, up_ref, down_ref))
-    ]
-    for c in loads:
-        c.start()
     for i in range(3):
         WT[128 * i + 112:128 * i + 128, :] = jnp.zeros((16, 2048), BF16)
 
-    for i, ref in enumerate((tok_ref, grd_ref)):
-        row = ref[...].astype(F32)
+    for i in range(2):
+        inputs[i].wait()
+        row = rows[i].astype(F32)
         for n in range(16):
             own32[16 * i + n:16 * i + n + 1, :] = row[:, 128 * n:128 * n + 128]
     G[0] = own32[...].astype(BF16)
@@ -160,10 +160,10 @@
                 Ag[first:first + 16, cols] = F[c, pl.ds(16 + n, 16, stride=32), :].astype(BF16)
 
     def forward(i):
-        rows = slice(64 * i, 64 * i + 64)
+        rws = slice(64 * i, 64 * i + 64)
         nt = (((1,), (1,)), ((), ()))
-        gu = lax.dot_general(At[rows, :], WT[0:256, :], nt, preferred_element_type=F32)
-        hg = lax.dot_general(Ag[rows, :], WT[256:384, :], nt, preferred_element_type=F32)
+        gu = lax.dot_general(At[rws, :], WT[0:256, :], nt, preferred_element_type=F32)
+        hg = lax.dot_general(Ag[rws, :], WT[256:384, :], nt, preferred_element_type=F32)
         part[i, :, :, 0:256] = gu.reshape(4, 16, 256)
         part[i, :, :, 256:384] = hg.reshape(4, 16, 128)
         for d in (1, 2, 3):
@@ -246,6 +246,12 @@
 
     relay(0)
     spread(0)
+    loads = [
+        pltpu.make_async_copy(ref, WT.at[pl.ds(128 * i, 112)], wl.at[i])
+        for i, ref in enumerate((gate_ref, up_ref, down_ref))
+    ]
+    for c in loads:
+        c.start()
     for k in (1, -1):
         z_wait(k, 0)
         relay(k)
@@ -333,18 +339,30 @@
         c.wait()
 
 
+def hand_over(*refs):
+    copies = [pltpu.make_async_copy(refs[i], refs[4 + i], refs[8].at[i]) for i in range(4)]
+    for c in copies:
+        c.start()
+    for c in copies:
+        c.wait()
+
+
 def body(tokens, out_grad, gate_weight, up_weight, down_weight):
     vmem = pl.BlockSpec(memory_space=pltpu.VMEM)
     anywhere = pl.BlockSpec(memory_space=pl.ANY)
     wide = jax.ShapeDtypeStruct((112, 2048), BF16)
+    shapes = (jax.ShapeDtypeStruct((1, 2048), BF16), wide, wide, wide)
     dma = lambda n: pltpu.SemaphoreType.DMA((n,))
-    in_grad, gate_grad, up_grad, down_grad = pl.pallas_call(
+    operands = (tokens, out_grad, gate_weight.T, up_weight.T, down_weight.T)
+    pinned = [pltpu.with_memory_space_constraint(v, pltpu.HBM) for v in operands]
+    results = pl.pallas_call(
         kernel,
         name="swiglu_backward",
-        out_shape=(jax.ShapeDtypeStruct((1, 2048), BF16), wide, wide, wide),
-        in_specs=[vmem, vmem, anywhere, anywhere, anywhere],
+        out_shape=shapes,
+        in_specs=[anywhere] * 5,
         out_specs=(vmem, anywhere, anywhere, anywhere),
         scratch_shapes=[
+            pltpu.VMEM((2, 1, 2048), BF16),
             pltpu.VMEM((32, 128), F32),
             pltpu.VMEM((256, 32, 128), BF16),
             pltpu.VMEM((2, 512, 128), F32),
@@ -365,12 +383,20 @@
             pltpu.VMEM((4, 16, 128), F32),
             pltpu.VMEM((384, 2048), BF16),
             dma(32), dma(32), dma(24), dma(24), dma(8), dma(8), dma(12), dma(12), dma(12), dma(12),
-            dma(8), dma(8), dma(12), dma(12), dma(len(RS)), dma(len(RS)), dma(4), dma(4), dma(3), dma(3),
+            dma(8), dma(8), dma(12), dma(12), dma(len(RS)), dma(len(RS)), dma(4), dma(4), dma(5), dma(3),
         ],
         compiler_params=pltpu.CompilerParams(
             collective_id=0, has_side_effects=True, vmem_limit_bytes=48 * 2 ** 20
         ),
-    )(tokens, out_grad, gate_weight.T, up_weight.T, down_weight.T)
+    )(*pinned)
+    in_grad, gate_grad, up_grad, down_grad = pl.pallas_call(
+        hand_over,
+        name="hand_over",
+        out_shape=shapes,
+        in_specs=[anywhere] * 4,
+        out_specs=(anywhere,) * 4,
+        scratch_shapes=[dma(4)],
+    )(*[pltpu.with_memory_space_constraint(v, pltpu.VMEM) for v in results])
     return in_grad, gate_grad.T, up_grad.T, down_grad.T
 
 

time: 89.1 us -> 82.1 us (0.921)
  the two profiles are of different devices: /device:TPU:8 before, /device:TPU:4 now
where the time goes in v2:
time: 82.1 us; the launch traced here: 81.9 us
  Pallas kernels  81.3 us (99%)
    pallas_call x1, Pallas kernels, body(): pl.pallas_call(kernel, name='swiglu_backward', out_shape=shapes, in_specs...  80.2 us

profile of v2, /device:TPU:4, one launch (start us, length us, event | category | flops | bytes accessed | tf_op | source)
XLA Modules:
  0.0 81.9 jit_solution(8267436142750568389)
XLA Ops:
  0.6 80.2 %swiglu_backward.1 = (bf16[1,2048]{1,0:T(2,128)(2,1)S(1)}, bf16[112,2048]{1,0:T(8,128)(2,1)S(1)}, bf16[112,2048]{1,0:T(8,128)(2,1)S(1)}, bf16[112,2048]{1,0:T(8,128)(2,1)S(1)}) custom-call(bf16[1,2048]{1,0:T(2,128)(2,1)} %tok_ref.1, bf16[1,2048]{1,0:T(2,128)(2,1)} %grd_ref.1, bf16[112,2048]{1,0:T(8,128)(2,1)} %bitcast.6, bf16[112,2048]{1,0:T(8,128)(2,1)} %bitcast.7, ...), custom_call_target="tpu_custom_call" | custom-call | tf_op jit(solution)/shard_map/swiglu_backward/pallas_call | solution.py:358
  80.8 1.1 %hand_over.1 = (bf16[1,2048]{1,0:T(2,128)(2,1)}, bf16[112,2048]{1,0:T(8,128)(2,1)}, bf16[112,2048]{1,0:T(8,128)(2,1)}, bf16[112,2048]{1,0:T(8,128)(2,1)}) custom-call(bf16[1,2048]{1,0:T(2,128)(2,1)S(1)} %get-tuple-element.12.refs_0_, bf16[112,2048]{1,0:T(8,128)(2,1)S(1)} %get-tuple-element.13.refs_1_, bf16[112,2048]{1,0:T(8,128)(2,1)S(1)} %get-tuple-element.14.refs_2_, ...), custom_call_target="tpu_custom_call" | custom-call | tf_op jit(solution)/shard_map/hand_over/pallas_call | solution.py:392

commit v3 on v2

--- a/solution.py
+++ b/solution.py
@@ -264,11 +264,11 @@
     for k in (1, -1):
         y_send(k)
     c_send(0)
+    for k in (2, -2):
+        y_send(k)
     for k in (3, -3):
         z_wait(k, 0)
         spread(k)
-    for k in (2, -2):
-        y_send(k)
     for k in (1, -1):
         c_send(k)
     for c in loads:
@@ -276,10 +276,10 @@
     for k in (0, 1):
         rows_in_place(k)
     forward(0)
+    for k in (3, -3, 4):
+        y_send(k)
     for k in (2, -2):
         c_send(k)
-    for k in (3, -3, 4):
-        y_send(k)
     for k in (-1, 2):
         rows_in_place(k)
     forward(1)

time: 82.1 us -> 80.7 us (0.983)
  the two profiles are of different devices: /device:TPU:4 before, /device:TPU:8 now
where the time goes in v3:
time: 80.7 us; the launch traced here: 80.5 us
  Pallas kernels  79.9 us (99%)
    pallas_call x1, Pallas kernels, body(): pl.pallas_call(kernel, name='swiglu_backward', out_shape=shapes, in_specs...  78.8 us

profile of v3, /device:TPU:8, one launch (start us, length us, event | category | flops | bytes accessed | tf_op | source)
XLA Modules:
  0.0 80.5 jit_solution(17534523404730784838)
XLA Ops:
  0.6 78.8 %swiglu_backward.1 = (bf16[1,2048]{1,0:T(2,128)(2,1)S(1)}, bf16[112,2048]{1,0:T(8,128)(2,1)S(1)}, bf16[112,2048]{1,0:T(8,128)(2,1)S(1)}, bf16[112,2048]{1,0:T(8,128)(2,1)S(1)}) custom-call(bf16[1,2048]{1,0:T(2,128)(2,1)} %tok_ref.1, bf16[1,2048]{1,0:T(2,128)(2,1)} %grd_ref.1, bf16[112,2048]{1,0:T(8,128)(2,1)} %bitcast.6, bf16[112,2048]{1,0:T(8,128)(2,1)} %bitcast.7, ...), custom_call_target="tpu_custom_call" | custom-call | tf_op jit(solution)/shard_map/swiglu_backward/pallas_call | solution.py:358
  79.4 1.1 %hand_over.1 = (bf16[1,2048]{1,0:T(2,128)(2,1)}, bf16[112,2048]{1,0:T(8,128)(2,1)}, bf16[112,2048]{1,0:T(8,128)(2,1)}, bf16[112,2048]{1,0:T(8,128)(2,1)}) custom-call(bf16[1,2048]{1,0:T(2,128)(2,1)S(1)} %get-tuple-element.12.refs_0_, bf16[112,2048]{1,0:T(8,128)(2,1)S(1)} %get-tuple-element.13.refs_1_, bf16[112,2048]{1,0:T(8,128)(2,1)S(1)} %get-tuple-element.14.refs_2_, ...), custom_call_target="tpu_custom_call" | custom-call | tf_op jit(solution)/shard_map/hand_over/pallas_call | solution.py:392
